TPU v7x, 32 devices: a whole 2x2x4 slice. The times are simulated.
32 devices in a mesh: dp: 8 (over z, x), cent: 4 (over y, core).
Axes of the slice: x: 2, y: 2, z: 4, core: 2. Of those that a mesh axis runs over, the one named last changes fastest.
Arguments:
- embeddings: bfloat16 [8192, 4096], P('dp'), may hold values from -15 to 15
- centroids: bfloat16 [8192, 4096], P('cent', 'dp'), may hold values from -12 to 12
Outputs:
- shares: bfloat16 [8192, 8192], P('dp', 'cent')
- new_centroids: bfloat16 [8192, 4096], P('cent', 'dp')
All inputs are finite; a program needn't handle non-finite values.
Results may differ from a plain program's by a relative error of at most 0.0034.
Values may be sent and summed in bfloat16 or wider, within the bound.
A program may use at most 128 MiB of HBM per device.

v0:
```python
import jax
import jax.numpy as jnp
from jax import lax
from jax.sharding import PartitionSpec as P

ROUNDS = 3


def on_device(embeddings, centroids):
    row_count = embeddings.shape[0]
    local_k = centroids.shape[0]
    rows_float = embeddings.astype(jnp.float32)
    normed = (
        rows_float * lax.rsqrt(jnp.sum(rows_float * rows_float, 1, keepdims=True) + 1e-06)
    ).astype(jnp.bfloat16)
    shard_piece = lax.all_gather(centroids, "dp", axis=1, tiled=True)
    piece_float = shard_piece.astype(jnp.float32)
    columns = normed
    scores = lax.dot_general(
        columns, shard_piece, (((1,), (1,)), ((), ())), preferred_element_type=jnp.float32
    )
    squares = jnp.sum(piece_float * piece_float, 1)
    scale = lax.rsqrt(squares + 1e-06)
    weights = jnp.exp(scores * scale[None, :] * 20.0)
    target = row_count * lax.axis_size("dp") / (local_k * lax.axis_size("cent"))
    for sweep in range(ROUNDS):
        column_sum = lax.psum(jnp.sum(weights, 0), "dp")
        weights = weights * (target / column_sum)[None, :]
        row_sum = lax.psum(jnp.sum(weights, 1), "cent")
        weights = weights / row_sum[:, None]
    shares = weights.astype(jnp.bfloat16)
    local_mass = jnp.sum(shares.astype(jnp.float32), 0)
    col_mass = lax.psum(local_mass, "dp")
    columns = embeddings
    sums = lax.psum_scatter(
        lax.dot_general(
            columns, shares, (((0,), (0,)), ((), ())), preferred_element_type=jnp.float32
        ),
        "dp",
        scatter_dimension=0,
        tiled=True,
    )
    new_centroids = (sums / col_mass[None, :]).T.astype(jnp.bfloat16)
    return (shares, new_centroids)


def solution(mesh):
    in_specs = (P("dp", None), P("cent", "dp"))
    out_specs = (P("dp", "cent"), P("cent", "dp"))
    return jax.shard_map(
        on_device, mesh=mesh, in_specs=in_specs, out_specs=out_specs, check_vma=False
    )
```

profile of v0, /device:TPU:0, one launch (start us, length us, event | category | flops | bytes accessed | tf_op | source)
XLA Modules:
  0.0 951.7 jit_solution(3530293727960485904)
XLA Ops:
  7.2 0.7 all-gather.2.cloned.1.call-update
  7.9 0.0 reduce-scatter.2.cloned.1.call-start
  7.9 5.1 fusion
  13.0 227.5 %all-gather.2.cloned.1.call-done = bf16[2048,4096]{1,0:T(8,128)(2,1)} async-done(((bf16[2048,512]{1,0:T(8,128)(2,1)}), bf16[2048,4096]{1,0:T(8,128)(2,1)}) %all-gather.2.cloned.1.call-update) | async-done | bytes 16777232 | tf_op jit(solution)/shard_map/all_gather | solution.py:16
  240.5 7.5 multiply_reduce_fusion
  248.1 3.1 copy-done
  251.2 22.8 %fusion.10 = (f32[2048]{0:T(1024)S(1)}, f32[1024,2048]{1,0:T(8,128)}) fusion(f32[2048]{0:T(1024)S(1)} %add_rsqrt_fusion, bf16[2048,4096]{1,0:T(8,128)(2,1)S(1)} %copy-done, bf16[1024,4096]{1,0:T(8,128)(2,1)} %param.2, f32[1024]{0:T(1024)S(1)} %add_rsqrt_fusion.1), kind=kOutput, calls=%fused_computation.25 | convolution fusion | flops 17198741504 | bytes 33574912 | tf_op jit(solution)/shard_map/dot_general | solution.py:19
  274.0 18.8 %psum.49 = f32[2048]{0:T(1024)S(1)} all-reduce(f32[2048]{0:T(1024)S(1)} %get-tuple-element.6), channel_id=1, replica_groups=mesh['dp'=8,'cent'=4] {'dp'}, use_global_device_ids=true, to_apply=%region_3.0 | all-reduce | flops 2048 | bytes 16384 | tf_op jit(solution)/shard_map/psum | solution.py:27
  292.8 4.0 multiply_reduce_fusion.3
  296.8 5.7 psum.50
  302.5 4.1 fusion.8
  306.6 17.9 %psum.51 = f32[2048]{0:T(1024)S(1)} all-reduce(f32[2048]{0:T(1024)S(1)} %fusion.8), channel_id=1, replica_groups=mesh['dp'=8,'cent'=4] {'dp'}, use_global_device_ids=true, to_apply=%region_7.0 | all-reduce | flops 2048 | bytes 16384 | tf_op jit(solution)/shard_map/psum | solution.py:27
  324.6 4.2 multiply_reduce_fusion.2
  328.8 5.7 psum.52
  334.5 6.7 fusion.9
  341.1 19.0 %psum.53 = f32[2048]{0:T(1024)S(1)} all-reduce(f32[2048]{0:T(1024)S(1)} %get-tuple-element.4), channel_id=1, replica_groups=mesh['dp'=8,'cent'=4] {'dp'}, use_global_device_ids=true, to_apply=%region_11.0 | all-reduce | flops 2048 | bytes 16384 | tf_op jit(solution)/shard_map/psum | solution.py:27
  360.1 4.0 multiply_reduce_fusion.1
  364.2 5.7 psum.54
  369.8 4.4 convert_reduce_fusion
  374.2 2.0 copy-done.1
  376.2 23.1 %convolution_bitcast_fusion = f32[4096,2048]{0,1:T(8,128)} fusion(bf16[1024,2048]{1,0:T(8,128)(2,1)S(1)} %get-tuple-element.3, bf16[1024,4096]{1,0:T(8,128)(2,1)} %param.2), kind=kOutput, calls=%fused_computation.3 | convolution fusion | flops 17179869184 | bytes 46137344 | tf_op jit(solution)/shard_map/dot_general | solution.py:36
  399.3 18.6 %psum.55 = f32[2048]{0:T(1024)S(1)} all-reduce(f32[2048]{0:T(1024)S(1)} %get-tuple-element.2), channel_id=1, replica_groups=mesh['dp'=8,'cent'=4] {'dp'}, use_global_device_ids=true, to_apply=%region_16.0 | all-reduce | flops 2048 | bytes 16384 | tf_op jit(solution)/shard_map/psum | solution.py:33
  418.0 523.0 %reduce-scatter.2.cloned.1.call-done = f32[512,2048]{0,1:T(8,128)} async-done(((f32[4096,2048]{0,1:T(8,128)}), f32[512,2048]{0,1:T(8,128)}) %reduce-scatter.2.cloned.1.call-update) | async-done | bytes 4194320 | tf_op jit(solution)/shard_map/reduce_scatter | solution.py:35
  941.0 3.9 fusion.7
  (9 shorter events, 0.1 us)
Async XLA Ops:
  7.2 233.4 %all-gather.2.cloned.1.call-start = ((), (), s32[]{:S(2)}) async-start(), calls=%async_computation.1 | async-start | bytes 18874368 | tf_op jit(solution)/shard_map/all_gather | solution.py:16
  7.9 933.1 %reduce-scatter.2.cloned.1.call-start = ((), (), s32[]{:S(2)}) async-start(), calls=%async_computation.2 | async-start | bytes 37748736 | tf_op jit(solution)/shard_map/reduce_scatter | solution.py:35
  240.5 10.7 %copy-start = (bf16[2048,4096]{1,0:T(8,128)(2,1)S(1)}, bf16[2048,4096]{1,0:T(8,128)(2,1)}, u32[]{:S(2)}) copy-start(bf16[2048,4096]{1,0:T(8,128)(2,1)} %all-gather.2.cloned.1.call-done) | copy-start | bytes 50331652
  374.2 2.0 copy-start.1
Sparse Core Ops, SparseCore 0:
  10.0 230.4 all-gather.1
  399.5 541.4 reduce-scatter.1
where the time goes:
time: 952 us
  waiting for transfers between devices  751 us (79%)
  blocking collectives  91.4 us (10%)
  matrix products  45.9 us (5%)
  other arithmetic  43.9 us (5%)
  between operations  14.1 us (1%)
    reduce_scatter x1, waiting for transfers between devices, on_device(): lax.psum_scatter(lax.dot_general(columns, shares, (((0,), (0,)), ((), ())...  523 us
    all_gather x1, waiting for transfers between devices, on_device(): shard_piece = lax.all_gather(centroids, 'dp', axis=1, tiled=True)  227 us
    psum x3, blocking collectives, on_device(): column_sum = lax.psum(jnp.sum(weights, 0), 'dp')  55.7 us
    dot_general x1, matrix products, on_device(): lax.dot_general(columns, shares, (((0,), (0,)), ((), ())), preferred_elem...  23.1 us
    dot_general x1, matrix products, on_device(): lax.dot_general(columns, shard_piece, (((1,), (1,)), ((), ())), preferred...  22.8 us
  transfers between devices with their start and end apart: 2, of which 2 were waited for; matrix products, arithmetic and copies ran while one was open for 1% of the time, Pallas kernels for 0%

commit v1 on v0

v1 whole, which is shorter than its diff:
```python
import functools

import jax
import jax.numpy as jnp
from jax import lax
from jax.experimental import pallas as pl
from jax.experimental.pallas import tpu as pltpu
from jax.sharding import PartitionSpec as P

ROUNDS = 3
LINE = 4
MESH = pl.DeviceIdType.MESH
F32 = jnp.float32
BF16 = jnp.bfloat16


def arrival_order(n, na, nb):
    table = []
    for me in range(n):
        a, b = divmod(me, nb)
        table.append(
            sorted(
                range(n),
                key=lambda s: (abs(s // nb - a) + abs(s % nb - b), abs(s % nb - b), s),
            )
        )
    return table


def pick(me, values):
    out = jnp.int32(values[0])
    for i, v in enumerate(values[1:], 1):
        out = jnp.where(me == i, jnp.int32(v), out)
    return out


def scores_kernel(
    n, nc, target, emb, cent, shares, mass, e_x, e_v, gath, w, sq, pr, rexp,
    col_out, col_in, row_out, row_in, loc_sem, snd, rcv, csnd, crcv, rsnd, rrcv,
    esnd, ercv, fsnd, frcv,
):
    me = lax.axis_index("dp")
    mc = lax.axis_index("cent")
    na = min(LINE, n)
    nb = n // na
    a, b = me // nb, me % nb
    rows = e_v.shape[0]
    local_k, feats = cent.shape
    half_k = local_k // 2
    tile = min(256, half_k)
    lanes = local_k // 128

    barrier = pltpu.get_barrier_semaphore()
    for k in range(1, n):
        pl.semaphore_signal(barrier, inc=1, device_id={"dp": lax.rem(me + k, n)}, device_id_type=MESH)
    for k in range(1, nc):
        pl.semaphore_signal(barrier, inc=1, device_id={"cent": lax.rem(mc + k, nc)}, device_id_type=MESH)
    pl.semaphore_wait(barrier, n - 1 + nc - 1)

    order = arrival_order(n, na, nb)

    def sends(e, src, h):
        sa, sb = src // nb, src % nb
        da, db = sa - a, sb - b
        ref = (cent if e == 0 else gath.at[src]).at[pl.ds(pl.multiple_of(h * half_k, half_k), half_k)]
        dst = gath.at[src].at[pl.ds(pl.multiple_of(h * half_k, half_k), half_k)]
        conds = (
            ((db == 0) & (da <= 0) & (a < na - 1), me + nb),
            ((db == 0) & (da >= 0) & (a > 0), me - nb),
            ((db <= 0) & (b < nb - 1), me + 1),
            ((db >= 0) & (b > 0), me - 1),
        )
        out = []
        for i, (cond, to) in enumerate(conds):
            out.append((cond, pltpu.make_async_remote_copy(
                src_ref=ref, dst_ref=dst, send_sem=snd.at[e, i, h], recv_sem=rcv.at[src, h],
                device_id={"dp": to}, device_id_type=MESH)))
        return out

    for h in range(2):
        for cond, copy in sends(0, me, h):
            @pl.when(cond)
            def _():
                copy.start()
    e_copy = pltpu.make_async_copy(emb, e_v, loc_sem.at[0])
    e_copy.start()
    own = pltpu.make_async_copy(cent, gath.at[me], loc_sem.at[1])
    own.start()
    e_copy.wait()

    chunk = 16

    @pl.loop(0, rows // chunk)
    def _(i):
        at = pl.ds(pl.multiple_of(i * chunk, chunk), chunk)
        x = e_v[at, :].astype(F32)
        s = jnp.sum(x * x, axis=1, keepdims=True)
        e_v[at, :] = (x * lax.rsqrt(s + 1e-06)).astype(BF16)

    own.wait()
    sq[...] = jnp.zeros_like(sq)
    ones = jnp.ones((8, feats), BF16)
    nt = (((1,), (1,)), ((), ()))

    for e in range(n):
        src = me if e == 0 else pick(me, [order[d][e] for d in range(n)])
        fcols = pl.ds(pl.multiple_of(src * feats, feats), feats)

        @pl.loop(0, 2)
        def _(h):
            if e > 0:
                outs = sends(e, src, h)
                outs[0][1].wait_recv()
                for cond, copy in outs:
                    @pl.when(cond)
                    def _():
                        copy.start()

            @pl.loop(0, half_k // tile)
            def _(t):
                k0 = pl.multiple_of(h * half_k + t * tile, tile)
                block = gath[src, pl.ds(k0, tile), :]
                part = lax.dot_general(e_v[:, fcols], block, nt, preferred_element_type=F32)
                if e == 0:
                    w[:, pl.ds(k0, tile)] = part
                else:
                    w[:, pl.ds(k0, tile)] += part
                bf = block.astype(F32)
                b2 = bf * bf
                hi = b2.astype(BF16)
                lo = (b2 - hi.astype(F32)).astype(BF16)
                sq[:, pl.ds(k0, tile)] += lax.dot_general(
                    ones, hi, nt, preferred_element_type=F32
                ) + lax.dot_general(ones, lo, nt, preferred_element_type=F32)

    half_rows = rows // 2
    mine = pl.ds(pl.multiple_of(lax.rem(mc, 2) * half_rows, half_rows), half_rows)
    e_copies, f_copies = [], []
    for k in range(1, nb):
        b2 = lax.rem(b + k, nb)
        for q in range(na):
            cols = pl.ds(pl.multiple_of((q * nb + b2) * feats, feats), feats)
            c = pltpu.make_async_remote_copy(
                src_ref=emb.at[mine, cols], dst_ref=e_x.at[k - 1, mine, pl.ds(q * feats, feats)],
                send_sem=esnd.at[k, q], recv_sem=ercv.at[k, q],
                device_id={"dp": a * nb + b2}, device_id_type=MESH)
            c.start()
            e_copies.append(c)
        f_copies.append(pltpu.make_async_remote_copy(
            src_ref=e_x.at[k - 1, mine], dst_ref=e_x.at[k - 1, mine],
            send_sem=fsnd.at[k], recv_sem=frcv.at[k],
            device_id={"cent": mc + 1 - 2 * lax.rem(mc, 2)}, device_id_type=MESH))

    def exchange_cols(r, part8):
        col_out[r] = jnp.sum(part8, axis=0, keepdims=True)
        copies = []
        for k in range(1, n):
            c = pltpu.make_async_remote_copy(
                src_ref=col_out.at[r], dst_ref=col_in.at[r, k], send_sem=csnd.at[r, k], recv_sem=crcv.at[r, k],
                device_id={"dp": lax.rem(me + k, n)}, device_id_type=MESH)
            c.start()
            copies.append(c)
        total = col_out[r]
        for k, c in enumerate(copies, 1):
            c.wait()
            total = total + col_in[r, k]
        return total

    def exchange_rows(r):
        for k in range(rows // 128):
            block = pr[k * 128:(k + 1) * 128, :]
            row_out[r, k:k + 1, :] = jnp.sum(block.T, axis=0, keepdims=True)
        copies = []
        for k in range(1, nc):
            c = pltpu.make_async_remote_copy(
                src_ref=row_out.at[r], dst_ref=row_in.at[r, k], send_sem=rsnd.at[r, k], recv_sem=rrcv.at[r, k],
                device_id={"cent": lax.rem(mc + k, nc)}, device_id_type=MESH)
            c.start()
            copies.append(c)
        total = row_out[r]
        for k, c in enumerate(copies, 1):
            c.wait()
            total = total + row_in[r, k]
        inv = 1.0 / total
        for k in range(rows // 128):
            rexp[k * 128:(k + 1) * 128, :] = jnp.broadcast_to(inv[k:k + 1, :], (128, 128)).T

    def wide(x):
        return jnp.concatenate([x] * lanes, axis=1)

    def narrow(x):
        out = x[:, :128]
        for t in range(1, lanes):
            out = out + x[:, t * 128:(t + 1) * 128]
        return out

    scale8 = lax.rsqrt(sq[...] + 1e-06) * 20.0
    zero8 = jnp.zeros((8, local_k), F32)

    def exp_pass(i, acc):
        at = pl.ds(pl.multiple_of(i * 8, 8), 8)
        x = jnp.exp(w[at, :] * scale8)
        w[at, :] = x
        return acc + x

    part8 = lax.fori_loop(0, rows // 8, exp_pass, zero8)
    for r in range(ROUNDS):
        if r > 0:
            def col_pass(i, acc):
                at = pl.ds(pl.multiple_of(i * 8, 8), 8)
                return acc + w[at, :] * wide(rexp[at, :])

            part8 = lax.fori_loop(0, rows // 8, col_pass, zero8)
        c8 = jnp.broadcast_to(target / exchange_cols(r, part8), (8, local_k))

        def row_pass(i, _):
            at = pl.ds(pl.multiple_of(i * 8, 8), 8)
            pr[at, :] = narrow(w[at, :] * c8)
            return 0

        lax.fori_loop(0, rows // 8, row_pass, 0)
        exchange_rows(r)

    for c in e_copies:
        c.wait()
    for c in f_copies:
        c.start()
    c16 = jnp.broadcast_to(c8[:1], (16, local_k))

    def share_pass(i, acc):
        at = pl.ds(pl.multiple_of(i * 16, 16), 16)
        s = (w[at, :] * wide(rexp[at, :]) * c16).astype(BF16)
        shares[at, :] = s
        s = s.astype(F32)
        return acc + (s[:8] + s[8:])

    part8 = lax.fori_loop(0, rows // 16, share_pass, zero8)
    mass[...] = exchange_cols(ROUNDS, part8)
    for c in f_copies:
        c.wait()

    for e in range(n):
        src = me if e == 0 else pick(me, [order[d][e] for d in range(n)])
        for h in range(2):
            for cond, copy in sends(e, src, h):
                @pl.when(cond)
                def _():
                    copy.wait_send()


def balanced(n, nc, embeddings, centroids):
    rows, width = embeddings.shape
    local_k, feats = centroids.shape
    target = rows * n / (local_k * nc)
    na = min(LINE, n)
    nb = n // na
    vmem = pl.BlockSpec(memory_space=pltpu.VMEM)
    dma = pltpu.SemaphoreType.DMA
    return pl.pallas_call(
        functools.partial(scores_kernel, n, nc, target),
        out_shape=(
            jax.ShapeDtypeStruct((rows, local_k), BF16),
            jax.ShapeDtypeStruct((1, local_k), F32),
            jax.ShapeDtypeStruct((nb - 1, rows, na * feats), BF16),
        ),
        in_specs=[pl.BlockSpec(memory_space=pl.ANY)] * 2,
        out_specs=(vmem, vmem, pl.BlockSpec(memory_space=pl.ANY)),
        scratch_shapes=[
            pltpu.VMEM((rows, width), BF16),
            pltpu.VMEM((n, local_k, feats), BF16),
            pltpu.VMEM((rows, local_k), F32),
            pltpu.VMEM((8, local_k), F32),
            pltpu.VMEM((rows, 128), F32),
            pltpu.VMEM((rows, 128), F32),
            pltpu.VMEM((ROUNDS + 1, 1, local_k), F32),
            pltpu.VMEM((ROUNDS + 1, n, 1, local_k), F32),
            pltpu.VMEM((ROUNDS, rows // 128, 128), F32),
            pltpu.VMEM((ROUNDS, nc, rows // 128, 128), F32),
            dma((2,)),
            dma((n, 4, 2)),
            dma((n, 2)),
            dma((ROUNDS + 1, n)),
            dma((ROUNDS + 1, n)),
            dma((ROUNDS, nc)),
            dma((ROUNDS, nc)),
            dma((nb, na)),
            dma((nb, na)),
            dma((nb,)),
            dma((nb,)),
        ],
        compiler_params=pltpu.CompilerParams(
            collective_id=0, has_side_effects=True, vmem_limit_bytes=58 * 2**20
        ),
        cost_estimate=pl.CostEstimate(
            flops=2 * rows * width * local_k, bytes_accessed=48 * 2**20, transcendentals=rows * local_k
        ),
    )(embeddings, centroids)


def means_kernel(
    n, chunk, emb, shares, mass, e_x, out, s_v, s_x, e_v, ex_v, st, slots, p_own, p_now,
    loc_sem, xsnd, xrcv, snd, rcv,
):
    me = lax.axis_index("dp")
    na = min(LINE, n)
    nb = n // na
    a, b = me // nb, me % nb
    rows, local_k = s_v.shape
    feats = out.shape[1]
    chunks = local_k // chunk

    barrier = pltpu.get_barrier_semaphore()
    for k in range(1, nb):
        pl.semaphore_signal(
            barrier, inc=1, device_id={"dp": a * nb + lax.rem(b + k, nb)}, device_id_type=MESH)

    @pl.when(a > 0)
    def _():
        pl.semaphore_signal(barrier, inc=1, device_id={"dp": me - nb}, device_id_type=MESH)

    @pl.when(a < na - 1)
    def _():
        pl.semaphore_signal(barrier, inc=1, device_id={"dp": me + nb}, device_id_type=MESH)

    neighbours = jnp.where(a > 0, 1, 0) + jnp.where(a < na - 1, 1, 0) + nb - 1
    pl.semaphore_wait(barrier, neighbours)

    def span(j):
        return pl.ds(pl.multiple_of(j * chunk, chunk), chunk)

    def share_copy(j, k):
        return pltpu.make_async_remote_copy(
            src_ref=shares.at[:, span(j)], dst_ref=s_x.at[k - 1, :, span(j)],
            send_sem=xsnd.at[j, k], recv_sem=xrcv.at[j, k],
            device_id={"dp": a * nb + lax.rem(b + k, nb)}, device_id_type=MESH)

    @pl.loop(0, chunks)
    def _(j):
        for k in range(1, nb):
            share_copy(j, k).start()

    loads = [pltpu.make_async_copy(shares, s_v, loc_sem.at[0]), pltpu.make_async_copy(e_x, ex_v, loc_sem.at[1])]
    for q in range(na):
        cols = pl.ds(pl.multiple_of((q * nb + b) * feats, feats), feats)
        loads.append(pltpu.make_async_copy(
            emb.at[:, cols], e_v.at[:, pl.ds(q * feats, feats)], loc_sem.at[2 + q]))
    for c in loads:
        c.start()
    for c in loads:
        c.wait()

    far_first = [sorted(range(na), key=lambda q: (-abs(q - m), q)) for m in range(na)]

    def up_copy(j, q):
        return pltpu.make_async_remote_copy(
            src_ref=slots.at[j, q], dst_ref=slots.at[j, q], send_sem=snd.at[j, q], recv_sem=rcv.at[j, q],
            device_id={"dp": me + nb}, device_id_type=MESH)

    def down_copy(j, q):
        to = jnp.where(q == a - 1, na, q)
        return pltpu.make_async_remote_copy(
            src_ref=slots.at[j, q], dst_ref=slots.at[j, to], send_sem=snd.at[j, q], recv_sem=rcv.at[j, to],
            device_id={"dp": me - nb}, device_id_type=MESH)

    def arrived(j, q):
        pltpu.make_async_remote_copy(
            src_ref=slots.at[j, q], dst_ref=slots.at[j, q], send_sem=snd.at[j, 0], recv_sem=rcv.at[j, q],
            device_id={"dp": me}, device_id_type=MESH).wait_recv()

    def send_chunk(j):
        for k in range(1, nb):
            share_copy(j, k).wait_recv()
        st[0] = s_v[:, span(j)].T
        for k in range(1, nb):
            st[k] = s_x[k - 1, :, span(j)].T
        for i in range(na):
            q = pick(a, [far_first[m][i] for m in range(na)])
            cols = pl.ds(pl.multiple_of(q * feats, feats), feats)
            p = jnp.dot(st[0], e_v[:, cols], preferred_element_type=F32)
            for k in range(1, nb):
                p = p + jnp.dot(st[k], ex_v[k - 1, :, cols], preferred_element_type=F32)
            if i == na - 1:
                p_own[j] = p
                continue
            p_now[...] = p
            up = q > a
            has_in = (up & (a > 0)) | ((q < a) & (a < na - 1))

            @pl.when(has_in)
            def _():
                arrived(j, q)
                p_now[...] += slots[j, q].astype(F32)

            slots[j, q] = p_now[...].astype(BF16)

            @pl.when(up)
            def _():
                up_copy(j, q).start()

            @pl.when(q < a)
            def _():
                down_copy(j, q).start()

    def finish_chunk(j):
        @pl.when(a > 0)
        def _():
            arrived(j, a)
            p_own[j] += slots[j, a].astype(F32)

        @pl.when(a < na - 1)
        def _():
            arrived(j, na)
            p_own[j] += slots[j, na].astype(F32)

        for t in range(chunk // 128):
            at = pl.ds(pl.multiple_of(j * chunk + t * 128, 128), 128)
            m = jnp.broadcast_to(mass[:, at], (128, 128)).T
            m = jnp.concatenate([m] * (feats // 128), axis=1)
            out[at, :] = (p_own[j, t * 128:(t + 1) * 128, :] / m).astype(BF16)

    late = min(2, chunks)

    @pl.loop(0, chunks)
    def _(j):
        send_chunk(j)

        @pl.when(j >= late)
        def _():
            finish_chunk(j - late)

    @pl.loop(chunks - late, chunks)
    def _(j):
        finish_chunk(j)

    @pl.loop(0, chunks)
    def _(j):
        for k in range(1, nb):
            share_copy(j, k).wait_send()
        for q in range(na):
            @pl.when(a < q)
            def _():
                up_copy(j, q).wait_send()

            @pl.when(a > q)
            def _():
                down_copy(j, q).wait_send()


def means(n, embeddings, shares, mass, e_x, feats):
    rows, local_k = shares.shape
    na = min(LINE, n)
    nb = n // na
    chunk = min(256, local_k)
    chunks = local_k // chunk
    vmem = pl.BlockSpec(memory_space=pltpu.VMEM)
    hbm = pl.BlockSpec(memory_space=pl.ANY)
    dma = pltpu.SemaphoreType.DMA
    return pl.pallas_call(
        functools.partial(means_kernel, n, chunk),
        out_shape=jax.ShapeDtypeStruct((local_k, feats), BF16),
        in_specs=[hbm, hbm, vmem, hbm],
        out_specs=vmem,
        scratch_shapes=[
            pltpu.VMEM((rows, local_k), BF16),
            pltpu.VMEM((nb - 1, rows, local_k), BF16),
            pltpu.VMEM((rows, na * feats), BF16),
            pltpu.VMEM((nb - 1, rows, na * feats), BF16),
            pltpu.VMEM((nb, chunk, rows), BF16),
            pltpu.VMEM((chunks, na + 1, chunk, feats), BF16),
            pltpu.VMEM((chunks, chunk, feats), F32),
            pltpu.VMEM((chunk, feats), F32),
            dma((2 + na,)),
            dma((chunks, nb)),
            dma((chunks, nb)),
            dma((chunks, na)),
            dma((chunks, na + 1)),
        ],
        compiler_params=pltpu.CompilerParams(
            collective_id=1, has_side_effects=True, vmem_limit_bytes=58 * 2**20
        ),
        cost_estimate=pl.CostEstimate(
            flops=2 * rows * n * feats * local_k, bytes_accessed=24 * 2**20, transcendentals=0
        ),
    )(embeddings, shares, mass, e_x)


def on_device(n, nc, embeddings, centroids):
    shares, mass, e_x = balanced(n, nc, embeddings, centroids)
    new_centroids = means(n, embeddings, shares, mass, e_x, centroids.shape[1])
    return (shares, new_centroids)


def solution(mesh):
    in_specs = (P("dp", None), P("cent", "dp"))
    out_specs = (P("dp", "cent"), P("cent", "dp"))
    return jax.shard_map(
        functools.partial(on_device, mesh.shape["dp"], mesh.shape["cent"]),
        mesh=mesh, in_specs=in_specs, out_specs=out_specs, check_vma=False,
    )
```

time: 952 us -> 436 us (0.46)
  waiting for transfers between devices: 751 us -> 0 us
  Pallas kernels: 0 us -> 431 us
  blocking collectives: 91.4 us -> 0 us
  matrix products: 45.9 us -> 0 us
  other arithmetic: 43.9 us -> 0 us
  between operations: 14.1 us -> 0.67 us
    reduce_scatter x1 -> x0, waiting for transfers between devices: 523 us -> none  [on_device(): lax.psum_scatter(lax.dot_general(columns, shares, (((0,), (0,)), ((), ())...]
    pallas_call x0 -> x2, Pallas kernels: none -> 431 us  [the longest x1 274 us: balanced(): pl.pallas_call(functools.partial(scores_kernel, n, nc, target), out_shape...]
    all_gather x1 -> x0, waiting for transfers between devices: 227 us -> none  [on_device(): shard_piece = lax.all_gather(centroids, 'dp', axis=1, tiled=True)]
    psum x7 -> x0, blocking collectives: 91.4 us -> none  [the longest x3 55.7 us: on_device(): column_sum = lax.psum(jnp.sum(weights, 0), 'dp')]
    dot_general x2 -> x0, matrix products: 45.9 us -> none  [the longest x1 23.1 us: on_device(): lax.dot_general(columns, shares, (((0,), (0,)), ((), ())), preferred_elem...]
    reduce_sum x8 -> x0, other arithmetic: 40 us -> none  [the longest x3 12.2 us: on_device(): row_sum = lax.psum(jnp.sum(weights, 1), 'cent')]
  transfers between devices with their start and end apart: 2 -> 0, of which waited for: 2 -> 0; matrix products, arithmetic and copies ran while one was open for 1% -> 0% of each run, Pallas kernels for 0% -> 0%
where the time goes in v1:
time: 436 us
  Pallas kernels  431 us (99%)
  local copies, waits for them, and re-layouts  4.4 us (1%)
    pallas_call x1, Pallas kernels, balanced(): pl.pallas_call(functools.partial(scores_kernel, n, nc, target), out_shape...  274 us
    pallas_call x1, Pallas kernels, means(): pl.pallas_call(functools.partial(means_kernel, n, chunk), out_shape=jax.S...  157 us

profile of v1, /device:TPU:0, one launch (start us, length us, event | category | flops | bytes accessed | tf_op | source)
XLA Modules:
  0.0 435.7 jit_solution(16122711917133419870)
XLA Ops:
  0.6 273.7 %shard_map.41 = (bf16[1024,2048]{1,0:T(8,128)(2,1)}, f32[1,2048]{1,0:T(1,128)}, bf16[1,1024,2048]{2,1,0:T(8,128)(2,1)}) custom-call(bf16[1024,4096]{1,0:T(8,128)(2,1)} %emb.3, bf16[2048,512]{1,0:T(8,128)(2,1)} %cent.1), custom_call_target="tpu_custom_call" | custom-call | flops 17179869184 | bytes 50331648 | tf_op jit(solution)/shard_map/pallas_call | solution.py:259
  274.4 0.0 copy-start
  274.4 156.9 %shard_map.42 = bf16[2048,512]{1,0:T(8,128)(2,1)} custom-call(bf16[1024,4096]{1,0:T(8,128)(2,1)} %emb.3, bf16[1024,2048]{1,0:T(8,128)(2,1)} %get-tuple-element.10.shares, f32[1,2048]{1,0:T(1,128)} %get-tuple-element.6.mass, bf16[1,1024,2048]{2,1,0:T(8,128)(2,1)} %get-tuple-element.7.e_x), custom_call_target="tpu_custom_call" | custom-call | flops 17179869184 | bytes 25165824 | tf_op jit(solution)/shard_map/pallas_call | solution.py:458
  431.3 0.0 copy-done
  431.3 0.0 copy-start.1
  431.3 2.1 copy.6
  433.4 0.9 copy-done.1
  434.3 1.3 copy.7
Async XLA Ops:
  274.4 156.9 %copy-start = (bf16[1024,2048]{1,0:T(8,128)(2,1)S(1)}, bf16[1024,2048]{1,0:T(8,128)(2,1)}, u32[]{:S(2)}) copy-start(bf16[1024,2048]{1,0:T(8,128)(2,1)} %get-tuple-element.10.shares) | copy-start | bytes 12582916
  431.3 3.1 copy-start.1

commit v2 on v1

--- a/solution.py
+++ b/solution.py
@@ -9,21 +9,30 @@
 
 ROUNDS = 3
 LINE = 4
+PIECES = 4
+DETOUR = 3
 MESH = pl.DeviceIdType.MESH
 F32 = jnp.float32
 BF16 = jnp.bfloat16
+
+
+def detour(a, na):
+    if isinstance(a, int):
+        return a + 1 if a < na // 2 else a - 1
+    return jnp.where(a < na // 2, a + 1, a - 1)
 
 
 def arrival_order(n, na, nb):
     table = []
     for me in range(n):
         a, b = divmod(me, nb)
-        table.append(
-            sorted(
-                range(n),
-                key=lambda s: (abs(s // nb - a) + abs(s % nb - b), abs(s % nb - b), s),
-            )
-        )
+
+        def key(s):
+            da, db = abs(s // nb - a), abs(s % nb - b)
+            late = nb == 2 and db > 0 and s // nb == detour(a, na)
+            return (da + 1.2 * db + (10 if late else 0), s)
+
+        table.append(sorted(range(n), key=key))
     return table
 
 
@@ -37,7 +46,7 @@
 def scores_kernel(
     n, nc, target, emb, cent, shares, mass, e_x, e_v, gath, w, sq, pr, rexp,
     col_out, col_in, row_out, row_in, loc_sem, snd, rcv, csnd, crcv, rsnd, rrcv,
-    esnd, ercv, fsnd, frcv,
+    esnd, ercv, fsnd, frcv, dsnd,
 ):
     me = lax.axis_index("dp")
     mc = lax.axis_index("cent")
@@ -46,8 +55,8 @@
     a, b = me // nb, me % nb
     rows = e_v.shape[0]
     local_k, feats = cent.shape
-    half_k = local_k // 2
-    tile = min(256, half_k)
+    piece = local_k // PIECES
+    tile = min(256, piece)
     lanes = local_k // 128
 
     barrier = pltpu.get_barrier_semaphore()
@@ -62,13 +71,17 @@
     def sends(e, src, h):
         sa, sb = src // nb, src % nb
         da, db = sa - a, sb - b
-        ref = (cent if e == 0 else gath.at[src]).at[pl.ds(pl.multiple_of(h * half_k, half_k), half_k)]
-        dst = gath.at[src].at[pl.ds(pl.multiple_of(h * half_k, half_k), half_k)]
+        at = pl.ds(pl.multiple_of(h * piece, piece), piece)
+        ref = (cent if e == 0 else gath.at[src]).at[at]
+        dst = gath.at[src].at[at]
+        across = jnp.bool_(True)
+        if nb == 2:
+            across = jnp.logical_not((h < DETOUR) & (sa == detour(a, na)))
         conds = (
             ((db == 0) & (da <= 0) & (a < na - 1), me + nb),
             ((db == 0) & (da >= 0) & (a > 0), me - nb),
-            ((db <= 0) & (b < nb - 1), me + 1),
-            ((db >= 0) & (b > 0), me - 1),
+            ((db <= 0) & (b < nb - 1) & across, me + 1),
+            ((db >= 0) & (b > 0) & across, me - 1),
         )
         out = []
         for i, (cond, to) in enumerate(conds):
@@ -77,11 +90,41 @@
                 device_id={"dp": to}, device_id_type=MESH)))
         return out
 
-    for h in range(2):
+    def detour_sends(h):
+        src = a * nb + 1 - b
+        at = pl.ds(pl.multiple_of(h * piece, piece), piece)
+        conds = (
+            ((a < na - 1) & (detour(a + 1, na) == a), me + nb),
+            ((a > 0) & (detour(a - 1, na) == a), me - nb),
+        )
+        return [(cond, pltpu.make_async_remote_copy(
+            src_ref=gath.at[src].at[at], dst_ref=gath.at[src].at[at], send_sem=dsnd.at[i, h], recv_sem=rcv.at[src, h],
+            device_id={"dp": to}, device_id_type=MESH)) for i, (cond, to) in enumerate(conds)]
+
+    for h in range(PIECES):
         for cond, copy in sends(0, me, h):
             @pl.when(cond)
             def _():
                 copy.start()
+    part_rows = rows // nc
+    mine = pl.ds(pl.multiple_of(mc * part_rows, part_rows), part_rows)
+    e_copies, f_copies = [], []
+    for k in range(1, nb):
+        b2 = lax.rem(b + k, nb)
+        for q in range(na):
+            cols = pl.ds(pl.multiple_of((q * nb + b2) * feats, feats), feats)
+            c = pltpu.make_async_remote_copy(
+                src_ref=emb.at[mine, cols], dst_ref=e_x.at[k - 1, mine, pl.ds(q * feats, feats)],
+                send_sem=esnd.at[k, q], recv_sem=ercv.at[k, q],
+                device_id={"dp": a * nb + b2}, device_id_type=MESH)
+            c.start()
+            e_copies.append(c)
+        for m in range(1, nc):
+            f_copies.append(pltpu.make_async_remote_copy(
+                src_ref=e_x.at[k - 1, mine], dst_ref=e_x.at[k - 1, mine],
+                send_sem=fsnd.at[k, m], recv_sem=frcv.at[k, m],
+                device_id={"cent": lax.rem(mc + m, nc)}, device_id_type=MESH))
+
     e_copy = pltpu.make_async_copy(emb, e_v, loc_sem.at[0])
     e_copy.start()
     own = pltpu.make_async_copy(cent, gath.at[me], loc_sem.at[1])
@@ -106,7 +149,7 @@
         src = me if e == 0 else pick(me, [order[d][e] for d in range(n)])
         fcols = pl.ds(pl.multiple_of(src * feats, feats), feats)
 
-        @pl.loop(0, 2)
+        @pl.loop(0, PIECES)
         def _(h):
             if e > 0:
                 outs = sends(e, src, h)
@@ -116,9 +159,9 @@
                     def _():
                         copy.start()
 
-            @pl.loop(0, half_k // tile)
+            @pl.loop(0, piece // tile)
             def _(t):
-                k0 = pl.multiple_of(h * half_k + t * tile, tile)
+                k0 = pl.multiple_of(h * piece + t * tile, tile)
                 block = gath[src, pl.ds(k0, tile), :]
                 part = lax.dot_general(e_v[:, fcols], block, nt, preferred_element_type=F32)
                 if e == 0:
@@ -133,23 +176,17 @@
                     ones, hi, nt, preferred_element_type=F32
                 ) + lax.dot_general(ones, lo, nt, preferred_element_type=F32)
 
-    half_rows = rows // 2
-    mine = pl.ds(pl.multiple_of(lax.rem(mc, 2) * half_rows, half_rows), half_rows)
-    e_copies, f_copies = [], []
-    for k in range(1, nb):
-        b2 = lax.rem(b + k, nb)
-        for q in range(na):
-            cols = pl.ds(pl.multiple_of((q * nb + b2) * feats, feats), feats)
-            c = pltpu.make_async_remote_copy(
-                src_ref=emb.at[mine, cols], dst_ref=e_x.at[k - 1, mine, pl.ds(q * feats, feats)],
-                send_sem=esnd.at[k, q], recv_sem=ercv.at[k, q],
-                device_id={"dp": a * nb + b2}, device_id_type=MESH)
-            c.start()
-            e_copies.append(c)
-        f_copies.append(pltpu.make_async_remote_copy(
-            src_ref=e_x.at[k - 1, mine], dst_ref=e_x.at[k - 1, mine],
-            send_sem=fsnd.at[k], recv_sem=frcv.at[k],
-            device_id={"cent": mc + 1 - 2 * lax.rem(mc, 2)}, device_id_type=MESH))
+        if e == n // 2 - 1:
+            for c in e_copies:
+                c.wait()
+            for c in f_copies:
+                c.start()
+        if nb == 2 and e == n // 2 + 1:
+            for h in range(DETOUR):
+                for cond, copy in detour_sends(h):
+                    @pl.when(cond)
+                    def _():
+                        copy.start()
 
     def exchange_cols(r, part8):
         col_out[r] = jnp.sum(part8, axis=0, keepdims=True)
@@ -221,10 +258,6 @@
         lax.fori_loop(0, rows // 8, row_pass, 0)
         exchange_rows(r)
 
-    for c in e_copies:
-        c.wait()
-    for c in f_copies:
-        c.start()
     c16 = jnp.broadcast_to(c8[:1], (16, local_k))
 
     def share_pass(i, acc):
@@ -241,8 +274,14 @@
 
     for e in range(n):
         src = me if e == 0 else pick(me, [order[d][e] for d in range(n)])
-        for h in range(2):
+        for h in range(PIECES):
             for cond, copy in sends(e, src, h):
+                @pl.when(cond)
+                def _():
+                    copy.wait_send()
+    if nb == 2:
+        for h in range(DETOUR):
+            for cond, copy in detour_sends(h):
                 @pl.when(cond)
                 def _():
                     copy.wait_send()
@@ -277,16 +316,17 @@
             pltpu.VMEM((ROUNDS, rows // 128, 128), F32),
             pltpu.VMEM((ROUNDS, nc, rows // 128, 128), F32),
             dma((2,)),
-            dma((n, 4, 2)),
-            dma((n, 2)),
+            dma((n, 4, PIECES)),
+            dma((n, PIECES)),
             dma((ROUNDS + 1, n)),
             dma((ROUNDS + 1, n)),
             dma((ROUNDS, nc)),
             dma((ROUNDS, nc)),
             dma((nb, na)),
             dma((nb, na)),
-            dma((nb,)),
-            dma((nb,)),
+            dma((nb, nc)),
+            dma((nb, nc)),
+            dma((2, PIECES)),
         ],
         compiler_params=pltpu.CompilerParams(
             collective_id=0, has_side_effects=True, vmem_limit_bytes=58 * 2**20

time: 436 us -> 390 us (0.89)
  Pallas kernels: 431 us -> 385 us
    pallas_call x1, Pallas kernels: 274 us -> 228 us  [balanced(): pl.pallas_call(functools.partial(scores_kernel, n, nc, target), out_shape...]
where the time goes in v2:
time: 390 us
  Pallas kernels  385 us (99%)
  local copies, waits for them, and re-layouts  4.4 us (1%)
    pallas_call x1, Pallas kernels, balanced(): pl.pallas_call(functools.partial(scores_kernel, n, nc, target), out_shape...  228 us
    pallas_call x1, Pallas kernels, means(): pl.pallas_call(functools.partial(means_kernel, n, chunk), out_shape=jax.S...  157 us

profile of v2, /device:TPU:0, one launch (start us, length us, event | category | flops | bytes accessed | tf_op | source)
XLA Modules:
  0.0 389.6 jit_solution(1709515365851263208)
XLA Ops:
  0.6 227.8 %shard_map.41 = (bf16[1024,2048]{1,0:T(8,128)(2,1)}, f32[1,2048]{1,0:T(1,128)}, bf16[1,1024,2048]{2,1,0:T(8,128)(2,1)}) custom-call(bf16[1024,4096]{1,0:T(8,128)(2,1)} %emb.3, bf16[2048,512]{1,0:T(8,128)(2,1)} %cent.1), custom_call_target="tpu_custom_call" | custom-call | flops 17179869184 | bytes 50331648 | tf_op jit(solution)/shard_map/pallas_call | solution.py:298
  228.4 0.0 copy-start
  228.4 156.8 %shard_map.42 = bf16[2048,512]{1,0:T(8,128)(2,1)} custom-call(bf16[1024,4096]{1,0:T(8,128)(2,1)} %emb.3, bf16[1024,2048]{1,0:T(8,128)(2,1)} %get-tuple-element.10.shares, f32[1,2048]{1,0:T(1,128)} %get-tuple-element.6.mass, bf16[1,1024,2048]{2,1,0:T(8,128)(2,1)} %get-tuple-element.7.e_x), custom_call_target="tpu_custom_call" | custom-call | flops 17179869184 | bytes 25165824 | tf_op jit(solution)/shard_map/pallas_call | solution.py:498
  385.2 0.0 copy-done
  385.2 0.0 copy-start.1
  385.2 2.1 copy.6
  387.4 0.9 copy-done.1
  388.3 1.3 copy.7
Async XLA Ops:
  228.4 156.8 %copy-start = (bf16[1024,2048]{1,0:T(8,128)(2,1)S(1)}, bf16[1024,2048]{1,0:T(8,128)(2,1)}, u32[]{:S(2)}) copy-start(bf16[1024,2048]{1,0:T(8,128)(2,1)} %get-tuple-element.10.shares) | copy-start | bytes 12582916
  385.2 3.1 copy-start.1

commit v3 on v2

v3 whole, which is shorter than its diff:
```python
import functools

import jax
import jax.numpy as jnp
from jax import lax
from jax.experimental import pallas as pl
from jax.experimental.pallas import tpu as pltpu
from jax.sharding import PartitionSpec as P

ROUNDS = 3
LINE = 4
PIECES = 4
CHUNK = 256
DETOUR = 3
MESH = pl.DeviceIdType.MESH
F32 = jnp.float32
BF16 = jnp.bfloat16


def detour(a, na):
    if isinstance(a, int):
        return a + 1 if a < na // 2 else a - 1
    return jnp.where(a < na // 2, a + 1, a - 1)


def arrival_order(n, na, nb):
    table = []
    for me in range(n):
        a, b = divmod(me, nb)

        def key(s):
            da, db = abs(s // nb - a), abs(s % nb - b)
            late = nb == 2 and db > 0 and s // nb == detour(a, na)
            return (da + 1.2 * db + (10 if late else 0), s)

        table.append(sorted(range(n), key=key))
    return table


def pick(me, values):
    out = jnp.int32(values[0])
    for i, v in enumerate(values[1:], 1):
        out = jnp.where(me == i, jnp.int32(v), out)
    return out


def step_kernel(
    n, nc, target, chunk, emb, cent, shares, out, e_v, gath, w, sq, pr, rexp,
    s_v, s_x, e_x, st, p_own, p_now, mass, col_now, col_out, col_in, row_out, row_in, loc_sem, snd, rcv, csnd, crcv, rsnd, rrcv,
    esnd, ercv, fsnd, frcv, dsnd, xsnd, xrcv, snd2, rcv2,
):
    me = lax.axis_index("dp")
    mc = lax.axis_index("cent")
    na = min(LINE, n)
    nb = n // na
    a, b = me // nb, me % nb
    rows = e_v.shape[0]
    local_k, feats = cent.shape
    piece = local_k // PIECES
    tile = min(256, piece)
    lanes = local_k // 128

    barrier = pltpu.get_barrier_semaphore()
    for k in range(1, n):
        pl.semaphore_signal(barrier, inc=1, device_id={"dp": lax.rem(me + k, n)}, device_id_type=MESH)
    for k in range(1, nc):
        pl.semaphore_signal(barrier, inc=1, device_id={"cent": lax.rem(mc + k, nc)}, device_id_type=MESH)
    pl.semaphore_wait(barrier, n - 1 + nc - 1)

    order = arrival_order(n, na, nb)

    def sends(e, src, h):
        sa, sb = src // nb, src % nb
        da, db = sa - a, sb - b
        dst = gath.at[pl.ds(pl.multiple_of(src * local_k + h * piece, piece), piece)]
        ref = cent.at[pl.ds(pl.multiple_of(h * piece, piece), piece)] if e == 0 else dst
        across = jnp.bool_(True)
        if nb == 2:
            across = jnp.logical_not((h < DETOUR) & (sa == detour(a, na)))
        conds = (
            ((db == 0) & (da <= 0) & (a < na - 1), me + nb),
            ((db == 0) & (da >= 0) & (a > 0), me - nb),
            ((db <= 0) & (b < nb - 1) & across, me + 1),
            ((db >= 0) & (b > 0) & across, me - 1),
        )
        out = []
        for i, (cond, to) in enumerate(conds):
            out.append((cond, pltpu.make_async_remote_copy(
                src_ref=ref, dst_ref=dst, send_sem=snd.at[e, i, h], recv_sem=rcv.at[src, h],
                device_id={"dp": to}, device_id_type=MESH)))
        return out

    def detour_sends(h):
        src = a * nb + 1 - b
        ref = gath.at[pl.ds(pl.multiple_of(src * local_k + h * piece, piece), piece)]
        conds = (
            ((a < na - 1) & (detour(a + 1, na) == a), me + nb),
            ((a > 0) & (detour(a - 1, na) == a), me - nb),
        )
        return [(cond, pltpu.make_async_remote_copy(
            src_ref=ref, dst_ref=ref, send_sem=dsnd.at[i, h], recv_sem=rcv.at[src, h],
            device_id={"dp": to}, device_id_type=MESH)) for i, (cond, to) in enumerate(conds)]

    for h in range(PIECES):
        for cond, copy in sends(0, me, h):
            @pl.when(cond)
            def _():
                copy.start()
    part_rows = rows // nc
    mine = pl.ds(pl.multiple_of(mc * part_rows, part_rows), part_rows)
    e_copies, f_copies = [], []
    for k in range(1, nb):
        b2 = lax.rem(b + k, nb)
        for q in range(na):
            cols = pl.ds(pl.multiple_of((q * nb + b2) * feats, feats), feats)
            c = pltpu.make_async_remote_copy(
                src_ref=emb.at[mine, cols], dst_ref=e_x.at[k - 1, mine, pl.ds(q * feats, feats)],
                send_sem=esnd.at[k, q], recv_sem=ercv.at[k, q],
                device_id={"dp": a * nb + b2}, device_id_type=MESH)
            c.start()
            e_copies.append(c)
        for m in range(1, nc):
            f_copies.append(pltpu.make_async_remote_copy(
                src_ref=e_x.at[k - 1, mine], dst_ref=e_x.at[k - 1, mine],
                send_sem=fsnd.at[k, m], recv_sem=frcv.at[k, m],
                device_id={"cent": lax.rem(mc + m, nc)}, device_id_type=MESH))

    e_copy = pltpu.make_async_copy(emb, e_v, loc_sem.at[0])
    e_copy.start()
    own = pltpu.make_async_copy(
        cent, gath.at[pl.ds(pl.multiple_of(me * local_k, local_k), local_k)], loc_sem.at[1])
    own.start()
    e_copy.wait()

    @pl.loop(0, rows // 16)
    def _(i):
        at = pl.ds(pl.multiple_of(i * 16, 16), 16)
        x = e_v[at, :].astype(F32)
        s = jnp.sum(x * x, axis=1, keepdims=True)
        e_v[at, :] = (x * lax.rsqrt(s + 1e-06)).astype(BF16)

    own.wait()
    sq[...] = jnp.zeros_like(sq)
    ones = jnp.ones((8, feats), BF16)
    nt = (((1,), (1,)), ((), ()))

    for e in range(n):
        src = me if e == 0 else pick(me, [order[d][e] for d in range(n)])
        fcols = pl.ds(pl.multiple_of(src * feats, feats), feats)

        @pl.loop(0, PIECES)
        def _(h):
            if e > 0:
                outs = sends(e, src, h)
                outs[0][1].wait_recv()
                for cond, copy in outs:
                    @pl.when(cond)
                    def _():
                        copy.start()

            @pl.loop(0, piece // tile)
            def _(t):
                k0 = pl.multiple_of(h * piece + t * tile, tile)
                block = gath[pl.ds(pl.multiple_of(src * local_k + k0, tile), tile), :]
                part = lax.dot_general(e_v[:, fcols], block, nt, preferred_element_type=F32)
                if e == 0:
                    w[:, pl.ds(k0, tile)] = part
                else:
                    w[:, pl.ds(k0, tile)] += part
                bf = block.astype(F32)
                b2 = bf * bf
                hi = b2.astype(BF16)
                lo = (b2 - hi.astype(F32)).astype(BF16)
                sq[:, pl.ds(k0, tile)] += lax.dot_general(
                    ones, hi, nt, preferred_element_type=F32
                ) + lax.dot_general(ones, lo, nt, preferred_element_type=F32)

        if e == n // 2 - 1:
            for c in e_copies:
                c.wait()
            for c in f_copies:
                c.start()
        if nb == 2 and e == n // 2 + 1:
            for h in range(DETOUR):
                for cond, copy in detour_sends(h):
                    @pl.when(cond)
                    def _():
                        copy.start()

    for e in range(n):
        src = me if e == 0 else pick(me, [order[d][e] for d in range(n)])
        for h in range(PIECES):
            for cond, copy in sends(e, src, h):
                @pl.when(cond)
                def _():
                    copy.wait_send()
    if nb == 2:
        for h in range(DETOUR):
            for cond, copy in detour_sends(h):
                @pl.when(cond)
                def _():
                    copy.wait_send()

    for c in f_copies:
        c.wait()
    e_copy.start()

    def col_copies(r):
        return [pltpu.make_async_remote_copy(
            src_ref=col_out.at[r], dst_ref=col_in.at[r, k], send_sem=csnd.at[r, k], recv_sem=crcv.at[r, k],
            device_id={"dp": lax.rem(me + k, n)}, device_id_type=MESH) for k in range(1, n)]

    def exchange_cols(r, part8):
        col_out[r] = jnp.sum(part8, axis=0, keepdims=True)
        copies = col_copies(r)
        for c in copies:
            c.start()
        total = col_out[r]
        for k, c in enumerate(copies, 1):
            c.wait()
            total = total + col_in[r, k]
        return total

    def exchange_rows(r):
        for k in range(rows // 128):
            block = pr[k * 128:(k + 1) * 128, :]
            row_out[r, k:k + 1, :] = jnp.sum(block.T, axis=0, keepdims=True)
        copies = []
        for k in range(1, nc):
            c = pltpu.make_async_remote_copy(
                src_ref=row_out.at[r], dst_ref=row_in.at[r, k], send_sem=rsnd.at[r, k], recv_sem=rrcv.at[r, k],
                device_id={"cent": lax.rem(mc + k, nc)}, device_id_type=MESH)
            c.start()
            copies.append(c)
        total = row_out[r]
        for k, c in enumerate(copies, 1):
            c.wait()
            total = total + row_in[r, k]
        inv = 1.0 / total
        for k in range(rows // 128):
            rexp[k * 128:(k + 1) * 128, :] = jnp.broadcast_to(inv[k:k + 1, :], (128, 128)).T

    def wide(x):
        return jnp.concatenate([x] * lanes, axis=1)

    def narrow(x):
        parts = [x[:, t * 128:(t + 1) * 128] for t in range(lanes)]
        while len(parts) > 1:
            half = [p + q for p, q in zip(parts[::2], parts[1::2])]
            parts = half + parts[len(half) * 2:]
        return parts[0]

    scale8 = lax.rsqrt(sq[...] + 1e-06) * 20.0
    zero8 = jnp.zeros((8, local_k), F32)

    def exp_pass(i, acc):
        at = pl.ds(pl.multiple_of(i * 8, 8), 8)
        x = jnp.exp(w[at, :] * scale8)
        w[at, :] = x
        return acc + x

    part8 = lax.fori_loop(0, rows // 8, exp_pass, zero8, unroll=4)
    for r in range(ROUNDS):
        if r > 0:
            def col_pass(i, acc):
                at = pl.ds(pl.multiple_of(i * 8, 8), 8)
                return acc + w[at, :] * wide(rexp[at, :])

            part8 = lax.fori_loop(0, rows // 8, col_pass, zero8, unroll=4)
        c8 = jnp.broadcast_to(target / exchange_cols(r, part8), (8, local_k))

        def row_pass(i, _):
            at = pl.ds(pl.multiple_of(i * 8, 8), 8)
            pr[at, :] = narrow(w[at, :] * c8)
            return 0

        lax.fori_loop(0, rows // 8, row_pass, 0, unroll=4)
        exchange_rows(r)

    chunks = local_k // chunk

    def span(j):
        return pl.ds(pl.multiple_of(j * chunk, chunk), chunk)

    def share_copy(j, k):
        return pltpu.make_async_remote_copy(
            src_ref=s_v.at[:, span(j)], dst_ref=s_x.at[k - 1, :, span(j)],
            send_sem=xsnd.at[j, k], recv_sem=xrcv.at[j, k],
            device_id={"dp": a * nb + lax.rem(b + k, nb)}, device_id_type=MESH)

    col_now[...] = c8[:1]
    last = ROUNDS

    @pl.loop(0, chunks)
    def _(j):
        c16 = jnp.broadcast_to(col_now[:, span(j)], (16, chunk))

        def share_pass(i, acc):
            at = pl.ds(pl.multiple_of(i * 16, 16), 16)
            r = rexp[at, :]
            x = (w[at, span(j)] * jnp.concatenate([r] * (chunk // 128), axis=1) * c16).astype(BF16)
            s_v[at, span(j)] = x
            x = x.astype(F32)
            return acc + (x[:8] + x[8:])

        part = lax.fori_loop(0, rows // 16, share_pass, jnp.zeros((8, chunk), F32), unroll=4)
        col_out[last, :, span(j)] = jnp.sum(part, axis=0, keepdims=True)
        for k in range(1, nb):
            share_copy(j, k).start()

    mass_copies = col_copies(last)
    for c in mass_copies:
        c.start()
    s_copy = pltpu.make_async_copy(s_v, shares, loc_sem.at[1])
    s_copy.start()
    e_copy.wait()

    def slot_at(j, q):
        return pl.ds(pl.multiple_of((j * (na + 1) + q) * chunk, chunk), chunk)

    def slot(j, q):
        return gath.at[slot_at(j, q)]

    far_first = [sorted(range(na), key=lambda q: (-abs(q - m), q)) for m in range(na)]

    def up_copy(j, q):
        return pltpu.make_async_remote_copy(
            src_ref=slot(j, q), dst_ref=slot(j, q), send_sem=snd2.at[j, q], recv_sem=rcv2.at[j, q],
            device_id={"dp": me + nb}, device_id_type=MESH)

    def down_copy(j, q):
        to = jnp.where(q == a - 1, na, q)
        return pltpu.make_async_remote_copy(
            src_ref=slot(j, q), dst_ref=slot(j, to), send_sem=snd2.at[j, q], recv_sem=rcv2.at[j, to],
            device_id={"dp": me - nb}, device_id_type=MESH)

    def arrived(j, q):
        pltpu.make_async_remote_copy(
            src_ref=slot(j, q), dst_ref=slot(j, q), send_sem=snd2.at[j, 0], recv_sem=rcv2.at[j, q],
            device_id={"dp": me}, device_id_type=MESH).wait_recv()

    def send_chunk(j):
        for k in range(1, nb):
            share_copy(j, k).wait_recv()
        st[0] = s_v[:, span(j)].T
        for k in range(1, nb):
            st[k] = s_x[k - 1, :, span(j)].T
        for i in range(na):
            q = pick(a, [far_first[m][i] for m in range(na)])
            cols = pl.ds(pl.multiple_of(q * feats, feats), feats)
            own_cols = pl.ds(pl.multiple_of((q * nb + b) * feats, feats), feats)
            p = jnp.dot(st[0], e_v[:, own_cols], preferred_element_type=F32)
            for k in range(1, nb):
                p = p + jnp.dot(st[k], e_x[k - 1, :, cols], preferred_element_type=F32)
            if i == na - 1:
                p_own[j] = p
                continue
            p_now[...] = p
            up = q > a
            has_in = (up & (a > 0)) | ((q < a) & (a < na - 1))

            @pl.when(has_in)
            def _():
                arrived(j, q)
                p_now[...] += gath[slot_at(j, q), :].astype(F32)

            gath[slot_at(j, q), :] = p_now[...].astype(BF16)

            @pl.when(up)
            def _():
                up_copy(j, q).start()

            @pl.when(q < a)
            def _():
                down_copy(j, q).start()

    def finish_chunk(j):
        @pl.when(a > 0)
        def _():
            arrived(j, a)
            p_own[j] += gath[slot_at(j, a), :].astype(F32)

        @pl.when(a < na - 1)
        def _():
            arrived(j, na)
            p_own[j] += gath[slot_at(j, na), :].astype(F32)

        for t in range(chunk // 128):
            at = pl.ds(pl.multiple_of(j * chunk + t * 128, 128), 128)
            m = jnp.broadcast_to(mass[:, at], (128, 128)).T
            m = jnp.concatenate([m] * (feats // 128), axis=1)
            out[at, :] = (p_own[j, t * 128:(t + 1) * 128, :] / m).astype(BF16)

    late = min(2, chunks - 1)

    @pl.loop(0, chunks)
    def _(j):
        send_chunk(j)

        @pl.when(j == late)
        def _():
            total = col_out[last]
            for k, c in enumerate(mass_copies, 1):
                c.wait()
                total = total + col_in[last, k]
            mass[...] = total

        @pl.when(j >= late)
        def _():
            finish_chunk(j - late)

    @pl.loop(chunks - late, chunks)
    def _(j):
        finish_chunk(j)

    @pl.loop(0, chunks)
    def _(j):
        for k in range(1, nb):
            share_copy(j, k).wait_send()
        for q in range(na):
            @pl.when(a < q)
            def _():
                up_copy(j, q).wait_send()

            @pl.when(a > q)
            def _():
                down_copy(j, q).wait_send()
    s_copy.wait()


def on_device(n, nc, embeddings, centroids):
    rows, width = embeddings.shape
    local_k, feats = centroids.shape
    target = rows * n / (local_k * nc)
    na = min(LINE, n)
    nb = n // na
    chunk = min(CHUNK, local_k)
    chunks = local_k // chunk
    vmem = pltpu.VMEM
    dma = pltpu.SemaphoreType.DMA
    hbm = pl.BlockSpec(memory_space=pl.ANY)
    return pl.pallas_call(
        functools.partial(step_kernel, n, nc, target, chunk),
        out_shape=(
            jax.ShapeDtypeStruct((rows, local_k), BF16),
            jax.ShapeDtypeStruct((local_k, feats), BF16),
        ),
        in_specs=[hbm, hbm],
        out_specs=(hbm, pl.BlockSpec(memory_space=pltpu.VMEM)),
        scratch_shapes=[
            vmem((rows, width), BF16),
            vmem((n * local_k, feats), BF16),
            vmem((rows, local_k), F32),
            vmem((8, local_k), F32),
            vmem((rows, 128), F32),
            vmem((rows, 128), F32),
            vmem((rows, local_k), BF16),
            vmem((nb - 1, rows, local_k), BF16),
            vmem((nb - 1, rows, na * feats), BF16),
            vmem((nb, chunk, rows), BF16),
            vmem((chunks, chunk, feats), F32),
            vmem((chunk, feats), F32),
            vmem((1, local_k), F32),
            vmem((1, local_k), F32),
            vmem((ROUNDS + 1, 1, local_k), F32),
            vmem((ROUNDS + 1, n, 1, local_k), F32),
            vmem((ROUNDS, rows // 128, 128), F32),
            vmem((ROUNDS, nc, rows // 128, 128), F32),
            dma((2,)),
            dma((n, 4, PIECES)),
            dma((n, PIECES)),
            dma((ROUNDS + 1, n)),
            dma((ROUNDS + 1, n)),
            dma((ROUNDS, nc)),
            dma((ROUNDS, nc)),
            dma((nb, na)),
            dma((nb, na)),
            dma((nb, nc)),
            dma((nb, nc)),
            dma((2, PIECES)),
            dma((chunks, nb)),
            dma((chunks, nb)),
            dma((chunks, na)),
            dma((chunks, na + 1)),
        ],
        compiler_params=pltpu.CompilerParams(
            collective_id=0, has_side_effects=True, vmem_limit_bytes=60 * 2**20
        ),
        cost_estimate=pl.CostEstimate(
            flops=4 * rows * width * local_k, bytes_accessed=48 * 2**20, transcendentals=rows * local_k
        ),
    )(embeddings, centroids)


def solution(mesh):
    in_specs = (P("dp", None), P("cent", "dp"))
    out_specs = (P("dp", "cent"), P("cent", "dp"))
    return jax.shard_map(
        functools.partial(on_device, mesh.shape["dp"], mesh.shape["cent"]),
        mesh=mesh, in_specs=in_specs, out_specs=out_specs, check_vma=False,
    )
```

time: 390 us -> 403 us (1.033)
  Pallas kernels: 385 us -> 396 us
    pallas_call x2 -> x1, Pallas kernels: 385 us -> 396 us  [on_device(): pl.pallas_call(functools.partial(step_kernel, n, nc, target, chunk), out_...]
where the time goes in v3:
time: 403 us
  Pallas kernels  396 us (98%)
  local copies, waits for them, and re-layouts  6.26 us (2%)
    pallas_call x1, Pallas kernels, on_device(): pl.pallas_call(functools.partial(step_kernel, n, nc, target, chunk), out_...  396 us

profile of v3, /device:TPU:0, one launch (start us, length us, event | category | flops | bytes accessed | tf_op | source)
XLA Modules:
  0.0 403.2 jit_solution(863573651377988916)
XLA Ops:
  0.6 396.2 %shard_map.41 = (bf16[1024,2048]{1,0:T(8,128)(2,1)}, bf16[2048,512]{1,0:T(8,128)(2,1)}) custom-call(bf16[1024,4096]{1,0:T(8,128)(2,1)} %emb.1, bf16[2048,512]{1,0:T(8,128)(2,1)} %cent.1), custom_call_target="tpu_custom_call" | custom-call | flops 34359738368 | bytes 50331648 | tf_op jit(solution)/shard_map/pallas_call | solution.py:442
  396.9 0.0 copy-start
  396.9 4.9 %copy.6 = bf16[1024,2048]{1,0:T(8,128)(2,1)} copy(bf16[1024,2048]{1,0:T(8,128)(2,1)} %get-tuple-element.4) | data formatting | bytes 8388608
  401.8 0.0 copy-done
  401.8 1.3 copy.7
Async XLA Ops:
  396.9 4.9 %copy-start = (bf16[2048,512]{1,0:T(8,128)(2,1)S(1)}, bf16[2048,512]{1,0:T(8,128)(2,1)}, u32[]{:S(2)}) copy-start(bf16[2048,512]{1,0:T(8,128)(2,1)} %get-tuple-element.5) | copy-start | bytes 6291460

commit v4 on v3

--- a/solution.py
+++ b/solution.py
@@ -305,12 +305,21 @@
 
         part = lax.fori_loop(0, rows // 16, share_pass, jnp.zeros((8, chunk), F32), unroll=4)
         col_out[last, :, span(j)] = jnp.sum(part, axis=0, keepdims=True)
-        for k in range(1, nb):
-            share_copy(j, k).start()
+
+        @pl.when(j == 0)
+        def _():
+            for k in range(1, nb):
+                share_copy(j, k).start()
 
     mass_copies = col_copies(last)
     for c in mass_copies:
         c.start()
+
+    @pl.loop(1, chunks)
+    def _(j):
+        for k in range(1, nb):
+            share_copy(j, k).start()
+
     s_copy = pltpu.make_async_copy(s_v, shares, loc_sem.at[1])
     s_copy.start()
     e_copy.wait()

time: 403 us -> 376 us (0.933)
  Pallas kernels: 396 us -> 369 us
    pallas_call x1, Pallas kernels: 396 us -> 369 us  [on_device(): pl.pallas_call(functools.partial(step_kernel, n, nc, target, chunk), out_...]
where the time goes in v4:
time: 376 us
  Pallas kernels  369 us (98%)
  local copies, waits for them, and re-layouts  6.26 us (2%)
    pallas_call x1, Pallas kernels, on_device(): pl.pallas_call(functools.partial(step_kernel, n, nc, target, chunk), out_...  369 us

profile of v4, /device:TPU:0, one launch (start us, length us, event | category | flops | bytes accessed | tf_op | source)
XLA Modules:
  0.0 376.3 jit_solution(16397324945618742221)
XLA Ops:
  0.6 369.4 %shard_map.41 = (bf16[1024,2048]{1,0:T(8,128)(2,1)}, bf16[2048,512]{1,0:T(8,128)(2,1)}) custom-call(bf16[1024,4096]{1,0:T(8,128)(2,1)} %emb.1, bf16[2048,512]{1,0:T(8,128)(2,1)} %cent.1), custom_call_target="tpu_custom_call" | custom-call | flops 34359738368 | bytes 50331648 | tf_op jit(solution)/shard_map/pallas_call | solution.py:451
  370.1 0.0 copy-start
  370.1 4.9 %copy.6 = bf16[1024,2048]{1,0:T(8,128)(2,1)} copy(bf16[1024,2048]{1,0:T(8,128)(2,1)} %get-tuple-element.4) | data formatting | bytes 8388608
  375.0 0.0 copy-done
  375.0 1.3 copy.7
Async XLA Ops:
  370.1 4.9 %copy-start = (bf16[2048,512]{1,0:T(8,128)(2,1)S(1)}, bf16[2048,512]{1,0:T(8,128)(2,1)}, u32[]{:S(2)}) copy-start(bf16[2048,512]{1,0:T(8,128)(2,1)} %get-tuple-element.5) | copy-start | bytes 6291460

commit v5 on v4

--- a/solution.py
+++ b/solution.py
@@ -141,39 +141,57 @@
 
     own.wait()
     sq[...] = jnp.zeros_like(sq)
-    ones = jnp.ones((8, feats), BF16)
     nt = (((1,), (1,)), ((), ()))
 
-    for e in range(n):
-        src = me if e == 0 else pick(me, [order[d][e] for d in range(n)])
+    def narrow(x):
+        parts = [x[:, t * 128:(t + 1) * 128] for t in range(x.shape[1] // 128)]
+        while len(parts) > 1:
+            half = [p + q for p, q in zip(parts[::2], parts[1::2])]
+            parts = half + parts[len(half) * 2:]
+        return parts[0]
+
+    def source(e):
+        return me if e == 0 else pick(me, [order[d][e] for d in range(n)])
+
+    def take(e, h):
+        src = source(e)
         fcols = pl.ds(pl.multiple_of(src * feats, feats), feats)
-
-        @pl.loop(0, PIECES)
-        def _(h):
-            if e > 0:
-                outs = sends(e, src, h)
-                outs[0][1].wait_recv()
-                for cond, copy in outs:
-                    @pl.when(cond)
-                    def _():
-                        copy.start()
-
-            @pl.loop(0, piece // tile)
-            def _(t):
-                k0 = pl.multiple_of(h * piece + t * tile, tile)
-                block = gath[pl.ds(pl.multiple_of(src * local_k + k0, tile), tile), :]
-                part = lax.dot_general(e_v[:, fcols], block, nt, preferred_element_type=F32)
-                if e == 0:
-                    w[:, pl.ds(k0, tile)] = part
-                else:
-                    w[:, pl.ds(k0, tile)] += part
-                bf = block.astype(F32)
-                b2 = bf * bf
-                hi = b2.astype(BF16)
-                lo = (b2 - hi.astype(F32)).astype(BF16)
-                sq[:, pl.ds(k0, tile)] += lax.dot_general(
-                    ones, hi, nt, preferred_element_type=F32
-                ) + lax.dot_general(ones, lo, nt, preferred_element_type=F32)
+        if e > 0:
+            outs = sends(e, src, h)
+            outs[0][1].wait_recv()
+            for cond, copy in outs:
+                @pl.when(cond)
+                def _():
+                    copy.start()
+
+        @pl.loop(0, piece // tile)
+        def _(t):
+            k0 = pl.multiple_of(h * piece + t * tile, tile)
+            block = gath[pl.ds(pl.multiple_of(src * local_k + k0, tile), tile), :]
+            part = lax.dot_general(e_v[:, fcols], block, nt, preferred_element_type=F32)
+            if e == 0:
+                w[:, pl.ds(k0, tile)] = part
+            else:
+                w[:, pl.ds(k0, tile)] += part
+            bf = block.astype(F32)
+            fold = narrow(bf * bf)
+            for u in range(tile // 128):
+                turned = fold[u * 128:(u + 1) * 128].T
+                eights = turned[:8]
+                for v in range(1, 16):
+                    eights = eights + turned[v * 8:(v + 1) * 8]
+                sq[:, pl.ds(pl.multiple_of(k0 + u * 128, 128), 128)] += eights
+
+    for e in range(n - 1):
+        if e < n - 2:
+            @pl.loop(0, PIECES)
+            def _(h):
+                take(e, h)
+        else:
+            @pl.loop(0, PIECES)
+            def _(h):
+                take(e, h)
+                take(e + 1, lax.rem(h + DETOUR, PIECES))
 
         if e == n // 2 - 1:
             for c in e_copies:
@@ -243,14 +261,8 @@
     def wide(x):
         return jnp.concatenate([x] * lanes, axis=1)
 
-    def narrow(x):
-        parts = [x[:, t * 128:(t + 1) * 128] for t in range(lanes)]
-        while len(parts) > 1:
-            half = [p + q for p, q in zip(parts[::2], parts[1::2])]
-            parts = half + parts[len(half) * 2:]
-        return parts[0]
-
-    scale8 = lax.rsqrt(sq[...] + 1e-06) * 20.0
+    scale8 = jnp.broadcast_to(
+        lax.rsqrt(jnp.sum(sq[...], axis=0, keepdims=True) + 1e-06) * 20.0, (8, local_k))
     zero8 = jnp.zeros((8, local_k), F32)
 
     def exp_pass(i, acc):

time: 376 us -> 373 us (level)
  no operation moved by 1% of the time
where the time goes in v5:
time: 373 us
  Pallas kernels  366 us (98%)
  local copies, waits for them, and re-layouts  6.26 us (2%)
    pallas_call x1, Pallas kernels, on_device(): pl.pallas_call(functools.partial(step_kernel, n, nc, target, chunk), out_...  366 us

profile of v5, /device:TPU:0, one launch (start us, length us, event | category | flops | bytes accessed | tf_op | source)
XLA Modules:
  0.0 373.3 jit_solution(4384735109862439524)
XLA Ops:
  0.6 366.4 %shard_map.41 = (bf16[1024,2048]{1,0:T(8,128)(2,1)}, bf16[2048,512]{1,0:T(8,128)(2,1)}) custom-call(bf16[1024,4096]{1,0:T(8,128)(2,1)} %emb.1, bf16[2048,512]{1,0:T(8,128)(2,1)} %cent.1), custom_call_target="tpu_custom_call" | custom-call | flops 34359738368 | bytes 50331648 | tf_op jit(solution)/shard_map/pallas_call | solution.py:463
  367.0 0.0 copy-start
  367.0 4.9 %copy.6 = bf16[1024,2048]{1,0:T(8,128)(2,1)} copy(bf16[1024,2048]{1,0:T(8,128)(2,1)} %get-tuple-element.4) | data formatting | bytes 8388608
  372.0 0.0 copy-done
  372.0 1.3 copy.7
Async XLA Ops:
  367.0 4.9 %copy-start = (bf16[2048,512]{1,0:T(8,128)(2,1)S(1)}, bf16[2048,512]{1,0:T(8,128)(2,1)}, u32[]{:S(2)}) copy-start(bf16[2048,512]{1,0:T(8,128)(2,1)} %get-tuple-element.5) | copy-start | bytes 6291460

commit v6 on v5

--- a/solution.py
+++ b/solution.py
@@ -10,7 +10,7 @@
 ROUNDS = 3
 LINE = 4
 PIECES = 4
-CHUNK = 256
+CHUNK = 128
 DETOUR = 3
 MESH = pl.DeviceIdType.MESH
 F32 = jnp.float32

time: 373 us -> 370 us (level)
  no operation moved by 1% of the time
where the time goes in v6:
time: 370 us
  Pallas kernels  363 us (98%)
  local copies, waits for them, and re-layouts  6.26 us (2%)
    pallas_call x1, Pallas kernels, on_device(): pl.pallas_call(functools.partial(step_kernel, n, nc, target, chunk), out_...  363 us

profile of v6, /device:TPU:0, one launch (start us, length us, event | category | flops | bytes accessed | tf_op | source)
XLA Modules:
  0.0 370.2 jit_solution(14374328645293141833)
XLA Ops:
  0.6 363.3 %shard_map.41 = (bf16[1024,2048]{1,0:T(8,128)(2,1)}, bf16[2048,512]{1,0:T(8,128)(2,1)}) custom-call(bf16[1024,4096]{1,0:T(8,128)(2,1)} %emb.1, bf16[2048,512]{1,0:T(8,128)(2,1)} %cent.1), custom_call_target="tpu_custom_call" | custom-call | flops 34359738368 | bytes 50331648 | tf_op jit(solution)/shard_map/pallas_call | solution.py:463
  364.0 0.0 copy-start
  364.0 4.9 %copy.6 = bf16[1024,2048]{1,0:T(8,128)(2,1)} copy(bf16[1024,2048]{1,0:T(8,128)(2,1)} %get-tuple-element.4) | data formatting | bytes 8388608
  368.9 0.0 copy-done
  368.9 1.3 copy.7
Async XLA Ops:
  364.0 4.9 %copy-start = (bf16[2048,512]{1,0:T(8,128)(2,1)S(1)}, bf16[2048,512]{1,0:T(8,128)(2,1)}, u32[]{:S(2)}) copy-start(bf16[2048,512]{1,0:T(8,128)(2,1)} %get-tuple-element.5) | copy-start | bytes 6291460
